TPU v7x, 32 devices: a whole 2x2x4 slice. The times are simulated.
32 devices in a mesh: ox: 4 (over y, core), oy: 8 (over z, x).
Axes of the slice: x: 2, y: 2, z: 4, core: 2. Of those that a mesh axis runs over, the one named last changes fastest.
Arguments:
- slip_rate: bfloat16 [4, 1024], P(None, ('ox', 'oy')), may hold values from -6 to 6
- green_kernel: bfloat16 [1024, 9, 8192], P(('ox', 'oy')), may hold values from -1 to 1
- intersection: int32 [32, 9], P(('ox', 'oy')), may hold values 0 or 1
- wet_mask: int32 [1024, 4096], P('ox', 'oy'), may hold values 0 or 1
- column_height: float32 [1024, 4096], P('ox', 'oy'), may hold values from 3 to 5
- east_flow: float32 [1024, 4096], P('ox', 'oy'), may hold values from -3 to 3
- north_flow: float32 [1024, 4096], P('ox', 'oy'), may hold values from -3 to 3
Outputs:
- height_out: float32 [1024, 4096], P('ox', 'oy')
- east_out: float32 [1024, 4096], P('ox', 'oy')
- north_out: float32 [1024, 4096], P('ox', 'oy')
All inputs are finite; a program needn't handle non-finite values. No bound on the sum of `intersection` or of `wet_mask` on one device may be relied on, other than what follows from the above.
Results may differ from a plain program's by a relative error of at most 0.0003.
Values sent between devices are 32-bit elements; how exact they have to be, the bound alone decides.
A program may use at most 64 MiB of HBM per device.

v0:
```python
import functools

import jax
import jax.numpy as jnp
from jax import lax
from jax.experimental import pallas as pl
from jax.experimental.pallas import tpu as pltpu
from jax.sharding import PartitionSpec as P

COARSE = 4
STRIP = 8
LANES = 128
PAD = 16

gravity = 1.0
ratio = 0.2
source = 0.05

MESH = pl.DeviceIdType.MESH
f32 = jnp.float32
bf16 = jnp.bfloat16


def iota(shape, dim):
    return lax.broadcasted_iota(jnp.int32, shape, dim)


def weights(slip_ref, cover_ref, steps, faults, a):
    rows = -(-3 * steps // PAD) * PAD
    wide = 3 * faults
    pick_step = (iota((rows, steps), 0) // 3 == iota((rows, steps), 1)).astype(bf16)
    pick_fault = (iota((faults, wide), 1) % faults == iota((faults, wide), 0)).astype(bf16)
    slips = jnp.dot(pick_step, slip_ref[...], preferred_element_type=f32).astype(bf16)
    slips = jnp.dot(slips, pick_fault, preferred_element_type=f32)
    slot = iota((rows, wide), 0) % 3
    cover = jnp.zeros((rows, wide), f32)
    for b in range(3):
        cover = jnp.where(slot == b, cover_ref[0, 3 * a + b].astype(f32), cover)
    return jnp.where(slot == iota((rows, wide), 1) // faults, slips * cover, 0.0).astype(bf16)


def flux_terms(h, m, n):
    inv = 1.0 / h
    u = m * inv
    v = n * inv
    pressure = 0.5 * gravity * h * h
    cross = m * v
    half = 0.5 * ratio
    fx = (half * m, half * (m * u + pressure), half * cross)
    fy = (half * n, half * cross, half * (n * v + pressure))
    quarter = (0.25 * h, 0.25 * m, 0.25 * n)
    return quarter, fx, fy


def kernel(
    n_ox, n_oy,
    slip_ref, green_ref, cover_ref, wet_hbm, h_hbm, m_hbm, n_hbm,
    h_out, m_out, n_out,
    green, part, state, wet, fine, spread, cols, halo_cols,
    route_x, summed, route_y, row_out, row_in, col_out, col_in, halo_rows,
    green_sem, load_sem, rx_send, rx_recv, ry_send, ry_recv, row_send, row_recv, col_send, col_recv,
):
    steps, faults = slip_ref.shape
    n_rows, n_cols = wet.shape
    up_rows, up_cols = n_rows // COARSE, n_cols // COARSE
    i, j = lax.axis_index("ox"), lax.axis_index("oy")
    near = (
        (i > 0, (i - 1, j)),
        (i < n_ox - 1, (i + 1, j)),
        (j > 0, (i, j - 1)),
        (j < n_oy - 1, (i, j + 1)),
    )

    loads = []
    for q, (src, dst) in enumerate((
        (h_hbm, state.at[0, 0, pl.ds(STRIP, n_rows)]),
        (m_hbm, state.at[0, 1, pl.ds(STRIP, n_rows)]),
        (n_hbm, state.at[0, 2, pl.ds(STRIP, n_rows)]),
        (wet_hbm, wet),
    )):
        loads.append(pltpu.make_async_copy(src, dst, load_sem.at[q]))
    for copy in loads:
        copy.start()
    chunks = green_sem.shape[1]
    width = green.shape[2] // chunks
    greens = {}
    for a in (2, 0, 1):
        for q in range(chunks):
            where = (pl.ds(3 * a, 3), slice(None), pl.ds(q * width, width))
            greens[a, q] = pltpu.make_async_copy(green_ref.at[where], green.at[where], green_sem.at[a, q])
            greens[a, q].start()

    barrier = pltpu.get_barrier_semaphore()
    for there, device in near:
        @pl.when(there)
        def _():
            pl.semaphore_signal(barrier, inc=1, device_id=device, device_id_type=MESH)

    zero_x = jnp.zeros(route_x.shape[2:], f32)
    zero_y = jnp.zeros(route_y.shape[2:], f32)
    for d in range(2):
        @pl.when(jnp.logical_not(near[d][0]))
        def _():
            for s in range(steps):
                route_x[s, d] = zero_x

        @pl.when(jnp.logical_not(near[2 + d][0]))
        def _():
            for s in range(steps):
                route_y[s, d] = zero_y

    coarse_of = iota((2 * up_cols, n_cols), 1) // COARSE
    spread[...] = (coarse_of == iota((2 * up_cols, n_cols), 0) % up_cols).astype(bf16)
    halo_cols[...] = jnp.zeros(halo_cols.shape, f32)
    lhs = [weights(slip_ref, cover_ref, steps, faults, a) for a in range(3)]

    pl.semaphore_wait(barrier, sum(there.astype(jnp.int32) for there, _ in near))

    def remote(src, dst, send, recv, d):
        return pltpu.make_async_remote_copy(
            src_ref=src, dst_ref=dst, send_sem=send, recv_sem=recv, device_id=near[d][1], device_id_type=MESH
        )

    def when_each(copies, what):
        for d, copy in copies:
            @pl.when(near[d ^ 1 if what == "wait_recv" else d][0])
            def _():
                getattr(copy, what)()

    def route_x_copies(s, sides=(0, 1)):
        rows = 3 * up_rows
        return [
            (d, remote(part.at[2 * d, pl.ds(s * rows, rows)], route_x.at[s, 1 - d], rx_send.at[s, d], rx_recv.at[s, 1 - d], d))
            for d in sides
        ]

    def route_y_copies(s):
        return [
            (2 + d, remote(summed.at[s, d], route_y.at[s, 1 - d], ry_send.at[s, d], ry_recv.at[s, 1 - d], 2 + d))
            for d in range(2)
        ]

    def row_copies(s):
        return [(d, remote(row_out.at[s, d], row_in.at[s, 1 - d], row_send.at[s, d], row_recv.at[s, 1 - d], d)) for d in range(2)]

    def col_copies(s):
        return [
            (2 + d, remote(col_out.at[s], col_in.at[s, 1 - d], col_send.at[s, d], col_recv.at[s, 1 - d], 2 + d))
            for d in range(2)
        ]

    lane = iota((STRIP, LANES), 1)
    first_lane = lane == 0
    last_lane = lane == LANES - 1
    row8 = iota((STRIP, n_cols), 0)

    def edge_columns(fields):
        packed = jnp.zeros((STRIP, LANES), f32)
        for c in range(3):
            first = fields[c][:, :LANES]
            last = fields[c][:, n_cols - LANES:]
            packed = jnp.where(lane == c, first if c == 0 else pltpu.roll(first, c, 1), packed)
            packed = jnp.where(lane == 3 + c, pltpu.roll(last, 4 + c, 1), packed)
        return packed

    def send_edges(s, buf):
        col_out[s] = jnp.transpose(cols[...])[:STRIP]
        for c in range(3):
            row_out[s, 0, pl.ds(c, 1)] = state[buf, c, pl.ds(STRIP, 1)]
            row_out[s, 1, pl.ds(c, 1)] = state[buf, c, pl.ds(STRIP + n_rows - 1, 1)]
        when_each(row_copies(s), "start")
        when_each(col_copies(s), "start")

    for copy in loads:
        copy.wait()

    def pack(k, carry):
        base = pl.multiple_of(k * STRIP, STRIP)
        cols[pl.ds(base, STRIP)] = edge_columns([state[0, c, pl.ds(base + STRIP, STRIP)] for c in range(3)])
        return carry

    lax.fori_loop(0, n_rows // STRIP, pack, 0)
    row_out[...] = jnp.zeros(row_out.shape, f32)
    send_edges(0, 0)

    for a in (2, 0, 1):
        for q in range(chunks):
            greens[a, q].wait()
            block = green[pl.ds(3 * a, 3), :, pl.ds(q * width, width)].reshape(3 * faults, width)
            out = jnp.dot(lhs[a], block, preferred_element_type=f32)
            for p in range(width // up_cols):
                row = q * (width // up_cols) + p
                part[a, pl.ds(row, out.shape[0], stride=up_rows), :] = out[:, p * up_cols:(p + 1) * up_cols]
        if a != 1:
            for s in range(steps):
                when_each(route_x_copies(s, (a // 2,)), "start")

    for s in range(steps):
        when_each(route_x_copies(s), "wait_recv")
        mine = part[1, pl.ds(s * 3 * up_rows, 3 * up_rows), :]
        total = mine + route_x[s, 0] + route_x[s, 1]
        summed[s, 0] = total[:up_rows]
        summed[s, 1] = total[2 * up_rows:]
        summed[s, 2] = total[up_rows:2 * up_rows]
        when_each(route_y_copies(s), "start")

    def receive_edges(s, buf):
        when_each(row_copies(s), "wait_recv")
        when_each(col_copies(s), "wait_recv")
        for d in range(2):
            halo_at = (STRIP - 1, STRIP + n_rows)[d]
            own = (STRIP, STRIP + n_rows - 1)[d]

            @pl.when(near[d][0])
            def _():
                for c in range(3):
                    state[buf, c, pl.ds(halo_at, 1)] = row_in[s, d, pl.ds(c, 1)]

            @pl.when(jnp.logical_not(near[d][0]))
            def _():
                for c in range(3):
                    state[buf, c, pl.ds(halo_at, 1)] = state[buf, c, pl.ds(own, 1)]

        @pl.when(near[3][0])
        def _():
            halo_rows[pl.ds(0, 3)] = col_in[s, 1, pl.ds(0, 3)]

        @pl.when(jnp.logical_not(near[3][0]))
        def _():
            halo_rows[pl.ds(0, 3)] = col_out[s, pl.ds(3, 3)]

        @pl.when(near[2][0])
        def _():
            halo_rows[pl.ds(3, 3)] = col_in[s, 0, pl.ds(3, 3)]

        @pl.when(jnp.logical_not(near[2][0]))
        def _():
            halo_rows[pl.ds(3, 3)] = col_out[s, pl.ds(0, 3)]

        right, _, right_y = flux_terms(*(halo_rows[pl.ds(c, 1)] for c in range(3)))
        left, _, left_y = flux_terms(*(halo_rows[pl.ds(3 + c, 1)] for c in range(3)))
        for c in range(3):
            halo_cols[pl.ds(c, 1), :n_rows] = right[c] - right_y[c]
            halo_cols[pl.ds(3 + c, 1), :n_rows] = left[c] + left_y[c]
        cols[...] = jnp.transpose(halo_cols[...])

    def shifted_pair(c, plus, minus, edge):
        n_blocks = n_cols // LANES
        ups, downs = [], []
        for b in range(n_blocks):
            ups.append(pltpu.roll(plus[:, b * LANES:(b + 1) * LANES], LANES - 1, 1))
            downs.append(pltpu.roll(minus[:, b * LANES:(b + 1) * LANES], 1, 1))
        result = []
        for b in range(n_blocks):
            after = ups[b + 1] if b < n_blocks - 1 else edge[:, c:c + 1]
            before = downs[b - 1] if b > 0 else edge[:, 3 + c:4 + c]
            result.append(jnp.where(last_lane, after, ups[b]) + jnp.where(first_lane, before, downs[b]))
        return jnp.concatenate(result, axis=1)

    def strip_terms(buf, k):
        base = pl.multiple_of(k * STRIP, STRIP)
        quarter, fx, fy = flux_terms(*(state[buf, c, pl.ds(base, STRIP)] for c in range(3)))
        up = [pltpu.roll(quarter[c] - fx[c], STRIP - 1, 0) for c in range(3)]
        down = [pltpu.roll(quarter[c] + fx[c], 1, 0) for c in range(3)]
        return quarter, fy, up, down

    def across(k, quarter, fy):
        edge = cols[pl.ds(pl.multiple_of((k - 1) * STRIP, STRIP), STRIP)]
        return [shifted_pair(c, quarter[c] - fy[c], quarter[c] + fy[c], edge) for c in range(3)]

    def step(s, buf):
        last = s == steps - 1
        n_strips = n_rows // STRIP

        def finish(k, acc, up, next_up):
            base = pl.multiple_of((k - 1) * STRIP, STRIP)
            dry = wet[pl.ds(base, STRIP)].astype(f32)
            values = [acc[c] + jnp.where(row8 == STRIP - 1, next_up[c], up[c]) for c in range(3)]
            lift = jnp.concatenate([fine[b, pl.ds(base, STRIP)] for b in range(n_cols // LANES)], axis=1)
            values = [values[0] + lift, values[1] * dry, values[2] * dry]
            for c in range(3):
                if last:
                    (h_out, m_out, n_out)[c][pl.ds(base, STRIP)] = values[c]
                else:
                    state[1 - buf, c, pl.ds(base + STRIP, STRIP)] = values[c]
            if not last:
                cols[pl.ds(base, STRIP)] = edge_columns(values)

        def start(k, down_before):
            quarter, fy, up, down = strip_terms(buf, k)
            sides = across(k, quarter, fy)
            acc = [sides[c] + jnp.where(row8 == 0, down_before[c], down[c]) for c in range(3)]
            return acc, up, down

        def body(k, carry):
            acc, up, down = carry
            new = start(k, down)
            finish(k - 1, acc, up, new[1])
            return new

        _, _, _, down = strip_terms(buf, 0)
        carry = start(1, down)
        acc, up, down = lax.fori_loop(2, n_strips + 1, body, carry)
        _, _, next_up, _ = strip_terms(buf, n_strips + 1)
        finish(n_strips, acc, up, next_up)

    for s in range(steps):
        buf = s % 2
        when_each(route_y_copies(s), "wait_recv")
        lift = source * (summed[s, 2] + route_y[s, 0] + route_y[s, 1])
        high = lift.astype(bf16)
        low = (lift - high.astype(f32)).astype(bf16)
        wide = jnp.dot(jnp.concatenate([high, low], axis=1), spread[...], preferred_element_type=f32)
        for b in range(n_cols // LANES):
            for t in range(COARSE):
                fine[b, pl.ds(t, up_rows, stride=COARSE), :] = wide[:, b * LANES:(b + 1) * LANES]
        receive_edges(s, buf)
        step(s, buf)
        if s < steps - 1:
            send_edges(s + 1, 1 - buf)

    for s in range(steps):
        when_each(route_x_copies(s), "wait_send")
        when_each(route_y_copies(s), "wait_send")
        when_each(row_copies(s), "wait_send")
        when_each(col_copies(s), "wait_send")


def shards(n_ox, n_oy, slip_rate, green_kernel, intersection, wet_mask, column_height, east_flow, north_flow):
    steps, faults = slip_rate.shape
    rows, cols = column_height.shape
    up_rows, up_cols = rows // COARSE, cols // COARSE
    part_rows = -(-3 * steps // PAD) * PAD * up_rows
    chunks = 4
    anywhere = pl.BlockSpec(memory_space=pl.ANY)
    vmem = pl.BlockSpec(memory_space=pltpu.VMEM)
    dma = pltpu.SemaphoreType.DMA
    return pl.pallas_call(
        functools.partial(kernel, n_ox, n_oy),
        out_shape=[jax.ShapeDtypeStruct((rows, cols), f32)] * 3,
        in_specs=[vmem, anywhere, pl.BlockSpec(memory_space=pltpu.SMEM)] + [anywhere] * 4,
        out_specs=[vmem] * 3,
        scratch_shapes=[
            pltpu.VMEM((9, faults, green_kernel.shape[2]), bf16),
            pltpu.VMEM((3, part_rows, up_cols), f32),
            pltpu.VMEM((2, 3, rows + 2 * STRIP, cols), f32),
            pltpu.VMEM((rows, cols), jnp.int32),
            pltpu.VMEM((cols // LANES, rows, LANES), f32),
            pltpu.VMEM((2 * up_cols, cols), bf16),
            pltpu.VMEM((rows, LANES), f32),
            pltpu.VMEM((LANES, rows), f32),
            pltpu.VMEM((steps, 2, 3 * up_rows, up_cols), f32),
            pltpu.VMEM((steps, 3, up_rows, up_cols), f32),
            pltpu.VMEM((steps, 2, up_rows, up_cols), f32),
            pltpu.VMEM((steps, 2, STRIP, cols), f32),
            pltpu.VMEM((steps, 2, STRIP, cols), f32),
            pltpu.VMEM((steps, STRIP, rows), f32),
            pltpu.VMEM((steps, 2, STRIP, rows), f32),
            pltpu.VMEM((STRIP, rows), f32),
            dma((3, chunks)),
            dma((4,)),
        ] + [dma((steps, 2))] * 8,
        compiler_params=pltpu.CompilerParams(
            collective_id=0, has_side_effects=True, vmem_limit_bytes=60 * 1024 * 1024
        ),
        cost_estimate=pl.CostEstimate(flops=400_000_000, bytes_accessed=16_000_000, transcendentals=0),
    )(slip_rate, green_kernel.transpose(1, 0, 2), intersection, wet_mask, column_height, east_flow, north_flow)


def solution(mesh):
    return jax.shard_map(
        functools.partial(shards, mesh.shape["ox"], mesh.shape["oy"]),
        mesh=mesh,
        in_specs=(
            P(None, ("ox", "oy")),
            P(("ox", "oy"), None, None),
            P(("ox", "oy"), None),
            P("ox", "oy"),
            P("ox", "oy"),
            P("ox", "oy"),
            P("ox", "oy"),
        ),
        out_specs=(P("ox", "oy"), P("ox", "oy"), P("ox", "oy")),
        check_vma=False,
    )
```

profile of v0, /device:TPU:1, one launch (start us, length us, event | category | flops | bytes accessed | tf_op | source)
XLA Modules:
  0.0 47.9 jit_solution(14851501960608830001)
XLA Ops:
  0.6 41.6 %shard_map.94 = (f32[256,512]{1,0:T(8,128)}, f32[256,512]{1,0:T(8,128)}, f32[256,512]{1,0:T(8,128)}) custom-call(bf16[4,32]{1,0:T(4,128)(2,1)} %slip_ref.1, bf16[9,32,8192]{2,1,0:T(8,128)(2,1)} %bitcast.1, s32[1,9]{1,0:T(1,128)} %cover_ref.1, s32[256,512]{1,0:T(8,128)} %wet_hbm.1, f32[256,512]{1,0:T(8,128)} %h_hbm.1, f32[256,512]{1,0:T(8,128)} %m_hbm.1, ...), custom_call_target="tpu_custom_call" | custom-call | flops 400000000 | bytes 16000000 | tf_op jit(solution)/shard_map/pallas_call | solution.py:338
  42.3 1.9 %copy.13 = f32[256,512]{1,0:T(8,128)} copy(f32[256,512]{1,0:T(8,128)} %get-tuple-element.6) | data formatting | bytes 1048576
  44.1 1.9 %copy.14 = f32[256,512]{1,0:T(8,128)} copy(f32[256,512]{1,0:T(8,128)} %get-tuple-element.7) | data formatting | bytes 1048576
  46.0 1.9 %copy.15 = f32[256,512]{1,0:T(8,128)} copy(f32[256,512]{1,0:T(8,128)} %get-tuple-element.8) | data formatting | bytes 1048576
where the time goes:
time: 48.2 us; the launch traced here: 47.9 us
  Pallas kernels  41.6 us (86%)
  local copies, waits for them, and re-layouts  5.6 us (12%)
  between operations  0.64 us (1%)
    pallas_call x1, Pallas kernels, shards(): pl.pallas_call(functools.partial(kernel, n_ox, n_oy), out_shape=[jax.Shap...  41.6 us
    unnamed x3, local copies, waits for them, and re-layouts  5.6 us

commit v1 on v0

v1 whole, which is shorter than its diff:
```python
import functools

import jax
import jax.numpy as jnp
from jax import lax
from jax.experimental import pallas as pl
from jax.experimental.pallas import tpu as pltpu
from jax.sharding import PartitionSpec as P

COARSE = 4
STRIP = 8
LANES = 128
PAD = 16
GROUP = 4
BLOCK = 32

gravity = 1.0
ratio = 0.2
source = 0.05

MESH = pl.DeviceIdType.MESH
f32 = jnp.float32
bf16 = jnp.bfloat16


def iota(shape, dim):
    return lax.broadcasted_iota(jnp.int32, shape, dim)


def weights(slip_ref, cover_ref, steps, faults, a):
    rows = -(-3 * steps // PAD) * PAD
    wide = 3 * faults
    pick_step = (iota((rows, steps), 0) // 3 == iota((rows, steps), 1)).astype(bf16)
    pick_fault = (iota((faults, wide), 1) % faults == iota((faults, wide), 0)).astype(bf16)
    slips = jnp.dot(pick_step, slip_ref[...], preferred_element_type=f32).astype(bf16)
    slips = jnp.dot(slips, pick_fault, preferred_element_type=f32)
    slot = iota((rows, wide), 0) % 3
    cover = jnp.zeros((rows, wide), f32)
    for b in range(3):
        cover = jnp.where(slot == b, cover_ref[0, 3 * a + b].astype(f32), cover)
    return jnp.where(slot == iota((rows, wide), 1) // faults, slips * cover, 0.0).astype(bf16)


def flux_terms(h, m, n):
    inv = 1.0 / h
    u = m * inv
    v = n * inv
    pressure = 0.5 * gravity * h * h
    cross = m * v
    half = 0.5 * ratio
    fx = (half * m, half * (m * u + pressure), half * cross)
    fy = (half * n, half * cross, half * (n * v + pressure))
    quarter = (0.25 * h, 0.25 * m, 0.25 * n)
    return quarter, fx, fy


def kernel(
    n_ox, n_oy,
    slip_ref, green_ref, cover_ref, wet_hbm, h_hbm, m_hbm, n_hbm,
    h_out, m_out, n_out,
    green, part, h_0, m_0, n_0, h_1, m_1, n_1, wet, fine, spread, edges, terms, terms_t,
    route_x, summed, route_y, row_out, row_in, col_out, col_in,
    green_sem, load_sem, rx_send, rx_recv, ry_send, ry_recv, row_send, row_recv, col_send, col_recv,
):
    steps, faults = slip_ref.shape
    n_rows, n_cols = wet.shape
    up_rows, up_cols = n_rows // COARSE, n_cols // COARSE
    i, j = lax.axis_index("ox"), lax.axis_index("oy")
    states = ((h_0, m_0, n_0), (h_1, m_1, n_1))
    outs = (h_out, m_out, n_out)
    near = (
        (i > 0, (i - 1, j)),
        (i < n_ox - 1, (i + 1, j)),
        (j > 0, (i, j - 1)),
        (j < n_oy - 1, (i, j + 1)),
    )

    loads = [
        pltpu.make_async_copy(src, dst, load_sem.at[q])
        for q, (src, dst) in enumerate(((h_hbm, h_0), (m_hbm, m_0), (n_hbm, n_0), (wet_hbm, wet)))
    ]
    chunks = green_sem.shape[1]
    width = green.shape[2] // chunks
    greens = {}
    for a in (2, 0, 1):
        for q in range(chunks):
            where = (pl.ds(3 * a, 3), slice(None), pl.ds(q * width, width))
            greens[a, q] = pltpu.make_async_copy(green_ref.at[where], green.at[where], green_sem.at[a, q])
            greens[a, q].start()
        if a == 2:
            for copy in loads:
                copy.start()

    barrier = pltpu.get_barrier_semaphore()
    for there, device in near:
        @pl.when(there)
        def _():
            pl.semaphore_signal(barrier, inc=1, device_id=device, device_id_type=MESH)

    zero_x = jnp.zeros(route_x.shape[2:], f32)
    zero_y = jnp.zeros(route_y.shape[2:], f32)
    for d in range(2):
        @pl.when(jnp.logical_not(near[d][0]))
        def _():
            for s in range(steps):
                route_x[s, d] = zero_x

        @pl.when(jnp.logical_not(near[2 + d][0]))
        def _():
            for s in range(steps):
                route_y[s, d] = zero_y

    coarse_of = iota((2 * up_cols, n_cols), 1) // COARSE
    spread[...] = (coarse_of == iota((2 * up_cols, n_cols), 0) % up_cols).astype(bf16)
    terms[...] = jnp.zeros(terms.shape, f32)
    row_out[...] = jnp.zeros(row_out.shape, f32)
    col_out[...] = jnp.zeros(col_out.shape, f32)
    lhs = [weights(slip_ref, cover_ref, steps, faults, a) for a in range(3)]

    pl.semaphore_wait(barrier, sum(there.astype(jnp.int32) for there, _ in near))

    def remote(src, dst, send, recv, d):
        return pltpu.make_async_remote_copy(
            src_ref=src, dst_ref=dst, send_sem=send, recv_sem=recv, device_id=near[d][1], device_id_type=MESH
        )

    def when_each(copies, what):
        for d, copy in copies:
            @pl.when(near[d ^ 1 if what == "wait_recv" else d][0])
            def _():
                getattr(copy, what)()

    def route_x_copies(s, sides=(0, 1)):
        rows = 3 * up_rows
        return [
            (d, remote(part.at[2 * d, pl.ds(s * rows, rows)], route_x.at[s, 1 - d], rx_send.at[s, d], rx_recv.at[s, 1 - d], d))
            for d in sides
        ]

    def route_y_copies(s):
        return [
            (2 + d, remote(summed.at[s, d], route_y.at[s, 1 - d], ry_send.at[s, d], ry_recv.at[s, 1 - d], 2 + d))
            for d in range(2)
        ]

    def row_copies(s):
        return [(d, remote(row_out.at[s, d], row_in.at[s, 1 - d], row_send.at[s, d], row_recv.at[s, 1 - d], d)) for d in range(2)]

    def col_copies(s):
        return [
            (2 + d, remote(col_out.at[s, d], col_in.at[s, 1 - d], col_send.at[s, d], col_recv.at[s, 1 - d], 2 + d))
            for d in range(2)
        ]

    first_block = pl.ds(0, LANES)
    last_block = pl.ds(n_cols - LANES, LANES)
    n_strips = n_rows // STRIP
    row8 = iota((STRIP, n_cols), 0)
    lane8 = iota((STRIP, LANES), 1)
    lane = iota((BLOCK, LANES), 1)

    def send_edges(s, state):
        for c in range(3):
            turned = jnp.transpose(edges[c])
            col_out[s, 0, pl.ds(c, 1)] = turned[:1]
            col_out[s, 1, pl.ds(c, 1)] = turned[LANES - 1:]
        when_each(col_copies(s), "start")

    def send_rows(s, state):
        for c in range(3):
            row_out[s, 0, pl.ds(c, 1)] = state[c][pl.ds(0, 1)]
            row_out[s, 1, pl.ds(c, 1)] = state[c][pl.ds(n_rows - 1, 1)]
        when_each(row_copies(s), "start")

    def matmul(a):
        for q in range(chunks):
            greens[a, q].wait()
            block = green[pl.ds(3 * a, 3), :, pl.ds(q * width, width)].reshape(3 * faults, width)
            out = jnp.dot(lhs[a], block, preferred_element_type=f32)
            for p in range(width // up_cols):
                row = q * (width // up_cols) + p
                part[a, pl.ds(row, out.shape[0], stride=up_rows), :] = out[:, p * up_cols:(p + 1) * up_cols]

    def pass_on(s):
        when_each(route_x_copies(s), "wait_recv")
        mine = part[1, pl.ds(s * 3 * up_rows, 3 * up_rows), :]
        total = mine + route_x[s, 0] + route_x[s, 1]
        summed[s, 0] = total[:up_rows]
        summed[s, 1] = total[2 * up_rows:]
        summed[s, 2] = total[up_rows:2 * up_rows]
        when_each(route_y_copies(s), "start")

    def lift_cells(s):
        when_each(route_y_copies(s), "wait_recv")
        lift = source * (summed[s, 2] + route_y[s, 0] + route_y[s, 1])
        high = lift.astype(bf16)
        low = (lift - high.astype(f32)).astype(bf16)
        wide = jnp.dot(jnp.concatenate([high, low], axis=1), spread[...], preferred_element_type=f32)
        for b in range(n_cols // LANES):
            for t in range(COARSE):
                fine[b, pl.ds(t, up_rows, stride=COARSE), :] = wide[:, b * LANES:(b + 1) * LANES]

    def beside(plus, minus):
        n_blocks = n_cols // LANES
        blocks = [slice(b * LANES, (b + 1) * LANES) for b in range(n_blocks)]
        after = [pltpu.roll(plus[:, block], LANES - 1, 1) for block in blocks] + [0.0]
        before = [0.0] + [pltpu.roll(minus[:, block], 1, 1) for block in blocks]
        return jnp.concatenate([
            jnp.where(lane8 == LANES - 1, after[b + 1], after[b]) + jnp.where(lane8 == 0, before[b], before[b + 1])
            for b in range(n_blocks)
        ], axis=1)

    def bulk(state, new):
        def start(base, down_before):
            quarter, fx, fy = flux_terms(*(field[pl.ds(base, STRIP)] for field in state))
            up = [pltpu.roll(quarter[c] - fx[c], STRIP - 1, 0) for c in range(3)]
            down = [pltpu.roll(quarter[c] + fx[c], 1, 0) for c in range(3)]
            sides = [beside(quarter[c] - fy[c], quarter[c] + fy[c]) for c in range(3)]
            acc = [sides[c] + jnp.where(row8 == 0, down_before[c], down[c]) for c in range(3)]
            return acc, up, down

        def store(base, acc, up, next_up):
            dry = wet[pl.ds(base, STRIP)].astype(f32)
            for c in range(3):
                value = acc[c] + jnp.where(row8 == STRIP - 1, next_up[c], up[c])
                new[c][pl.ds(base, STRIP)] = value * dry if c > 0 else value

        def group(base, carry):
            for u in range(GROUP):
                now = start(base + u * STRIP, carry[2])
                if carry[0] is not None:
                    store(base + (u - 1) * STRIP, carry[0], carry[1], now[1])
                carry = now
            return carry

        zero = jnp.zeros((STRIP, n_cols), f32)
        carry = group(0, (None, None, [zero] * 3))
        carry = lax.fori_loop(
            1, n_strips // GROUP, lambda t, carry: group(pl.multiple_of(t * GROUP * STRIP, GROUP * STRIP), carry), carry
        )
        store(n_rows - STRIP, carry[0], carry[1], [zero] * 3)

    def receive(s):
        when_each(row_copies(s), "wait_recv")
        when_each(col_copies(s), "wait_recv")
        for d in range(2):
            @pl.when(jnp.logical_not(near[d][0]))
            def _():
                row_in[s, d] = row_out[s, d]

            @pl.when(jnp.logical_not(near[2 + d][0]))
            def _():
                col_in[s, d] = col_out[s, d]

        for d in range(2):
            quarter, _, fy = flux_terms(*(col_in[s, d, pl.ds(c, 1)] for c in range(3)))
            for c in range(3):
                terms[c, pl.ds(d * (LANES - 1), 1)] = quarter[c] - fy[c] if d else quarter[c] + fy[c]
        for c in range(3):
            terms_t[c] = jnp.transpose(terms[c])

    def finish(s, new):
        for d in range(2):
            row = pl.ds(d * (n_rows - 1), 1)
            quarter, fx, _ = flux_terms(*(row_in[s, d, pl.ds(c, 1)] for c in range(3)))
            dry = wet[row].astype(f32)
            for c in range(3):
                term = quarter[c] - fx[c] if d else quarter[c] + fx[c]
                new[c][row] = new[c][row] + (term * dry if c > 0 else term)

        def body(t, carry):
            where = pl.ds(pl.multiple_of(t * BLOCK, BLOCK), BLOCK)
            dry_first = wet[where, first_block].astype(f32)
            dry_last = wet[where, last_block].astype(f32)
            for b in range(n_cols // LANES):
                block = pl.ds(b * LANES, LANES)
                new[0][where, block] = new[0][where, block] + fine[b, where]
            for c in range(3):
                term = terms_t[c, where]
                left = jnp.where(lane == 0, term, 0.0)
                right = jnp.where(lane == LANES - 1, term, 0.0)
                first = new[c][where, first_block] + (left * dry_first if c > 0 else left)
                last = new[c][where, last_block] + (right * dry_last if c > 0 else right)
                new[c][where, first_block] = first
                new[c][where, last_block] = last
                edges[c, where] = jnp.where(lane == 0, first, last)
            return carry

        lax.fori_loop(0, n_rows // BLOCK, body, 0)

    for a in (2, 0):
        matmul(a)
        for s in range(steps):
            when_each(route_x_copies(s, (a // 2,)), "start")

    for copy in loads:
        copy.wait()
    for c in range(3):
        edges[c] = jnp.where(iota((n_rows, LANES), 1) == 0, states[0][c][:, first_block], states[0][c][:, last_block])
    send_rows(0, states[0])
    send_edges(0, states[0])

    matmul(1)
    pass_on(0)
    for s in range(steps):
        state = states[s % 2]
        new = outs if s == steps - 1 else states[1 - s % 2]
        bulk(state, new)
        if s == 0:
            for later in range(1, steps):
                pass_on(later)
        lift_cells(s)
        receive(s)
        finish(s, new)
        if s < steps - 1:
            send_rows(s + 1, new)
            send_edges(s + 1, new)

    for s in range(steps):
        when_each(route_x_copies(s), "wait_send")
        when_each(route_y_copies(s), "wait_send")
        when_each(row_copies(s), "wait_send")
        when_each(col_copies(s), "wait_send")


def write_out(h, m, n, h_hbm, m_hbm, n_hbm, sems):
    copies = [
        pltpu.make_async_copy(src, dst, sems.at[q])
        for q, (src, dst) in enumerate(((h, h_hbm), (m, m_hbm), (n, n_hbm)))
    ]
    for copy in copies:
        copy.start()
    for copy in copies:
        copy.wait()


def shards(n_ox, n_oy, slip_rate, green_kernel, intersection, wet_mask, column_height, east_flow, north_flow):
    steps, faults = slip_rate.shape
    rows, cols = column_height.shape
    up_rows, up_cols = rows // COARSE, cols // COARSE
    part_rows = -(-3 * steps // PAD) * PAD * up_rows
    chunks = 4
    hbm = pl.BlockSpec(memory_space=pltpu.HBM)
    vmem = pl.BlockSpec(memory_space=pltpu.VMEM)
    dma = pltpu.SemaphoreType.DMA
    fields = [jax.ShapeDtypeStruct((rows, cols), f32)] * 3
    result = pl.pallas_call(
        functools.partial(kernel, n_ox, n_oy),
        out_shape=fields,
        in_specs=[vmem, hbm, pl.BlockSpec(memory_space=pltpu.SMEM)] + [hbm] * 4,
        out_specs=[vmem] * 3,
        scratch_shapes=[
            pltpu.VMEM((9, faults, green_kernel.shape[2]), bf16),
            pltpu.VMEM((3, part_rows, up_cols), f32),
        ] + [pltpu.VMEM((rows, cols), f32)] * 6 + [
            pltpu.VMEM((rows, cols), jnp.int32),
            pltpu.VMEM((cols // LANES, rows, LANES), f32),
            pltpu.VMEM((2 * up_cols, cols), bf16),
            pltpu.VMEM((3, rows, LANES), f32),
            pltpu.VMEM((3, LANES, rows), f32),
            pltpu.VMEM((3, rows, LANES), f32),
            pltpu.VMEM((steps, 2, 3 * up_rows, up_cols), f32),
            pltpu.VMEM((steps, 3, up_rows, up_cols), f32),
            pltpu.VMEM((steps, 2, up_rows, up_cols), f32),
            pltpu.VMEM((steps, 2, STRIP, cols), f32),
            pltpu.VMEM((steps, 2, STRIP, cols), f32),
            pltpu.VMEM((steps, 2, STRIP, rows), f32),
            pltpu.VMEM((steps, 2, STRIP, rows), f32),
            dma((3, chunks)),
            dma((4,)),
        ] + [dma((steps, 2))] * 8,
        compiler_params=pltpu.CompilerParams(
            collective_id=0, has_side_effects=True, vmem_limit_bytes=52 * 1024 * 1024
        ),
        cost_estimate=pl.CostEstimate(flops=400_000_000, bytes_accessed=16_000_000, transcendentals=0),
    )(slip_rate, green_kernel.transpose(1, 0, 2), intersection, wet_mask, column_height, east_flow, north_flow)
    return pl.pallas_call(
        write_out,
        out_shape=fields,
        in_specs=[vmem] * 3,
        out_specs=[hbm] * 3,
        scratch_shapes=[dma((3,))],
        cost_estimate=pl.CostEstimate(flops=0, bytes_accessed=6 * rows * cols * 4, transcendentals=0),
    )(*result)


def solution(mesh):
    return jax.shard_map(
        functools.partial(shards, mesh.shape["ox"], mesh.shape["oy"]),
        mesh=mesh,
        in_specs=(
            P(None, ("ox", "oy")),
            P(("ox", "oy"), None, None),
            P(("ox", "oy"), None),
            P("ox", "oy"),
            P("ox", "oy"),
            P("ox", "oy"),
            P("ox", "oy"),
        ),
        out_specs=(P("ox", "oy"), P("ox", "oy"), P("ox", "oy")),
        check_vma=False,
    )
```

time: 48.2 us -> 31.4 us (0.65)
  Pallas kernels: 41.6 us -> 26.9 us
  local copies, waits for them, and re-layouts: 5.6 us -> 3.7 us
    pallas_call x1 -> x2, Pallas kernels: 41.6 us -> 26.9 us  [the longest x1 24.3 us: shards(): pl.pallas_call(functools.partial(kernel, n_ox, n_oy), out_shape=fields, i...]
    unnamed x3 -> x10, local copies, waits for them, and re-layouts: 5.6 us -> 3.7 us
where the time goes in v1:
time: 31.4 us; the launch traced here: 31.2 us
  Pallas kernels  26.9 us (86%)
  local copies, waits for them, and re-layouts  3.7 us (12%)
  between operations  0.66 us (2%)
    pallas_call x1, Pallas kernels, shards(): pl.pallas_call(functools.partial(kernel, n_ox, n_oy), out_shape=fields, i...  24.3 us
    unnamed x10, local copies, waits for them, and re-layouts  3.7 us
    pallas_call x1, Pallas kernels, shards(): pl.pallas_call(write_out, out_shape=fields, in_specs=[vmem] * 3, out_spec...  2.52 us

profile of v1, /device:TPU:1, one launch (start us, length us, event | category | flops | bytes accessed | tf_op | source)
XLA Modules:
  0.0 31.2 jit_solution(8534802917163664756)
XLA Ops:
  0.6 0.0 copy-start.3
  0.6 0.7 %copy-done.3 = bf16[4,32]{1,0:T(4,128)(2,1)S(1)} copy-done((bf16[4,32]{1,0:T(4,128)(2,1)S(1)}, bf16[4,32]{1,0:T(4,128)(2,1)}, u32[]{:S(2)}) %copy-start.3) | copy-done | bytes 280
  1.3 0.0 copy-start.4
  1.3 0.7 %copy-done.4 = s32[1,9]{1,0:T(1,128)S(1)} copy-done((s32[1,9]{1,0:T(1,128)S(1)}, s32[1,9]{1,0:T(1,128)}, u32[]{:S(2)}) %copy-start.4) | copy-done | bytes 60
  2.0 24.3 %shard_map.94 = (f32[256,512]{1,0:T(8,128)S(1)}, f32[256,512]{1,0:T(8,128)S(1)}, f32[256,512]{1,0:T(8,128)S(1)}) custom-call(bf16[4,32]{1,0:T(4,128)(2,1)S(1)} %copy-done.3, bf16[9,32,8192]{2,1,0:T(8,128)(2,1)} %bitcast.1, s32[1,9]{1,0:T(1,128)S(1)} %copy-done.4, s32[256,512]{1,0:T(8,128)} %wet_hbm.1, f32[256,512]{1,0:T(8,128)} %h_hbm.1, f32[256,512]{1,0:T(8,128)} %m_hbm.1, ...), custom_call_target="tpu_custom_call" | custom-call | flops 400000000 | bytes 16000000 | tf_op jit(solution)/shard_map/pallas_call | solution.py:347
  26.3 0.0 copy-start
  26.3 0.8 %copy-done = f32[256,512]{1,0:T(8,128)} copy-done((f32[256,512]{1,0:T(8,128)}, f32[256,512]{1,0:T(8,128)S(1)}, u32[]{:S(2)}) %copy-start) | copy-done | bytes 524312
  27.1 0.0 copy-start.1
  27.1 0.8 %copy-done.1 = f32[256,512]{1,0:T(8,128)} copy-done((f32[256,512]{1,0:T(8,128)}, f32[256,512]{1,0:T(8,128)S(1)}, u32[]{:S(2)}) %copy-start.1) | copy-done | bytes 524312
  27.9 0.0 copy-start.2
  27.9 0.8 %copy-done.2 = f32[256,512]{1,0:T(8,128)} copy-done((f32[256,512]{1,0:T(8,128)}, f32[256,512]{1,0:T(8,128)S(1)}, u32[]{:S(2)}) %copy-start.2) | copy-done | bytes 524312
  28.7 2.5 %shard_map.95 = (f32[256,512]{1,0:T(8,128)}, f32[256,512]{1,0:T(8,128)}, f32[256,512]{1,0:T(8,128)}) custom-call(f32[256,512]{1,0:T(8,128)} %copy-done, f32[256,512]{1,0:T(8,128)} %copy-done.1, f32[256,512]{1,0:T(8,128)} %copy-done.2), custom_call_target="tpu_custom_call" | custom-call | bytes 3145728 | tf_op jit(solution)/shard_map/pallas_call | solution.py:377
Async XLA Ops:
  0.6 0.7 %copy-start.3 = (bf16[4,32]{1,0:T(4,128)(2,1)S(1)}, bf16[4,32]{1,0:T(4,128)(2,1)}, u32[]{:S(2)}) copy-start(bf16[4,32]{1,0:T(4,128)(2,1)} %slip_ref.1) | copy-start | bytes 772
  1.3 0.7 %copy-start.4 = (s32[1,9]{1,0:T(1,128)S(1)}, s32[1,9]{1,0:T(1,128)}, u32[]{:S(2)}) copy-start(s32[1,9]{1,0:T(1,128)} %cover_ref.1) | copy-start | bytes 112
  26.3 0.8 %copy-start = (f32[256,512]{1,0:T(8,128)}, f32[256,512]{1,0:T(8,128)S(1)}, u32[]{:S(2)}) copy-start(f32[256,512]{1,0:T(8,128)S(1)} %get-tuple-element.6.h) | copy-start | bytes 1572868
  27.1 0.8 %copy-start.1 = (f32[256,512]{1,0:T(8,128)}, f32[256,512]{1,0:T(8,128)S(1)}, u32[]{:S(2)}) copy-start(f32[256,512]{1,0:T(8,128)S(1)} %get-tuple-element.7.m) | copy-start | bytes 1572868
  27.9 0.8 %copy-start.2 = (f32[256,512]{1,0:T(8,128)}, f32[256,512]{1,0:T(8,128)S(1)}, u32[]{:S(2)}) copy-start(f32[256,512]{1,0:T(8,128)S(1)} %get-tuple-element.8.n) | copy-start | bytes 1572868

commit v2 on v1

--- a/solution.py
+++ b/solution.py
@@ -11,7 +11,7 @@
 STRIP = 8
 LANES = 128
 PAD = 16
-GROUP = 4
+GROUP = 8
 BLOCK = 32
 
 gravity = 1.0
@@ -42,16 +42,14 @@
 
 
 def flux_terms(h, m, n):
-    inv = 1.0 / h
-    u = m * inv
-    v = n * inv
-    pressure = 0.5 * gravity * h * h
-    cross = m * v
     half = 0.5 * ratio
-    fx = (half * m, half * (m * u + pressure), half * cross)
-    fy = (half * n, half * cross, half * (n * v + pressure))
-    quarter = (0.25 * h, 0.25 * m, 0.25 * n)
-    return quarter, fx, fy
+    guess = pl.reciprocal(h, approx=True)
+    inv = guess * (2.0 - h * guess)
+    u, v = m * inv, n * inv
+    east, north = half * m, half * n
+    pressure = (0.5 * gravity * half * h) * h
+    cross = east * v
+    return (0.25 * h, 0.25 * m, 0.25 * n), (east, east * u + pressure, cross), (north, cross, north * v + pressure)
 
 
 def kernel(
@@ -159,7 +157,7 @@
     lane8 = iota((STRIP, LANES), 1)
     lane = iota((BLOCK, LANES), 1)
 
-    def send_edges(s, state):
+    def send_edges(s):
         for c in range(3):
             turned = jnp.transpose(edges[c])
             col_out[s, 0, pl.ds(c, 1)] = turned[:1]
@@ -283,7 +281,8 @@
                 last = new[c][where, last_block] + (right * dry_last if c > 0 else right)
                 new[c][where, first_block] = first
                 new[c][where, last_block] = last
-                edges[c, where] = jnp.where(lane == 0, first, last)
+                if s < steps - 1:
+                    edges[c, where] = jnp.where(lane == 0, first, last)
             return carry
 
         lax.fori_loop(0, n_rows // BLOCK, body, 0)
@@ -298,7 +297,7 @@
     for c in range(3):
         edges[c] = jnp.where(iota((n_rows, LANES), 1) == 0, states[0][c][:, first_block], states[0][c][:, last_block])
     send_rows(0, states[0])
-    send_edges(0, states[0])
+    send_edges(0)
 
     matmul(1)
     pass_on(0)
@@ -314,7 +313,7 @@
         finish(s, new)
         if s < steps - 1:
             send_rows(s + 1, new)
-            send_edges(s + 1, new)
+            send_edges(s + 1)
 
     for s in range(steps):
         when_each(route_x_copies(s), "wait_send")
@@ -380,6 +379,7 @@
         in_specs=[vmem] * 3,
         out_specs=[hbm] * 3,
         scratch_shapes=[dma((3,))],
+        compiler_params=pltpu.CompilerParams(vmem_limit_bytes=4 * 1024 * 1024),
         cost_estimate=pl.CostEstimate(flops=0, bytes_accessed=6 * rows * cols * 4, transcendentals=0),
     )(*result)
 

time: 31.4 us -> 27.4 us (0.87)
  local copies, waits for them, and re-layouts: 3.7 us -> 1.33 us
  Pallas kernels: 26.9 us -> 25.3 us
    unnamed x10 -> x4, local copies, waits for them, and re-layouts: 3.7 us -> 1.33 us
    pallas_call x1, Pallas kernels: 2.52 us -> 1.17 us  [shards(): pl.pallas_call(write_out, out_shape=fields, in_specs=[vmem] * 3, out_spec...]
where the time goes in v2:
time: 27.4 us; the launch traced here: 27.3 us
  Pallas kernels  25.3 us (92%)
  local copies, waits for them, and re-layouts  1.33 us (5%)
  between operations  0.65 us (2%)
    pallas_call x1, Pallas kernels, shards(): pl.pallas_call(functools.partial(kernel, n_ox, n_oy), out_shape=fields, i...  24.1 us
    unnamed x4, local copies, waits for them, and re-layouts  1.33 us
    pallas_call x1, Pallas kernels, shards(): pl.pallas_call(write_out, out_shape=fields, in_specs=[vmem] * 3, out_spec...  1.17 us

profile of v2, /device:TPU:1, one launch (start us, length us, event | category | flops | bytes accessed | tf_op | source)
XLA Modules:
  0.0 27.3 jit_solution(13095955037711428548)
XLA Ops:
  0.6 0.0 copy-start
  0.6 0.7 %copy-done = bf16[4,32]{1,0:T(4,128)(2,1)S(1)} copy-done((bf16[4,32]{1,0:T(4,128)(2,1)S(1)}, bf16[4,32]{1,0:T(4,128)(2,1)}, u32[]{:S(2)}) %copy-start) | copy-done | bytes 280
  1.3 0.0 copy-start.1
  1.3 0.7 %copy-done.1 = s32[1,9]{1,0:T(1,128)S(1)} copy-done((s32[1,9]{1,0:T(1,128)S(1)}, s32[1,9]{1,0:T(1,128)}, u32[]{:S(2)}) %copy-start.1) | copy-done | bytes 60
  2.0 24.1 %shard_map.94 = (f32[256,512]{1,0:T(8,128)S(1)}, f32[256,512]{1,0:T(8,128)S(1)}, f32[256,512]{1,0:T(8,128)S(1)}) custom-call(bf16[4,32]{1,0:T(4,128)(2,1)S(1)} %copy-done, bf16[9,32,8192]{2,1,0:T(8,128)(2,1)} %bitcast.1, s32[1,9]{1,0:T(1,128)S(1)} %copy-done.1, s32[256,512]{1,0:T(8,128)} %wet_hbm.1, f32[256,512]{1,0:T(8,128)} %h_hbm.1, f32[256,512]{1,0:T(8,128)} %m_hbm.1, ...), custom_call_target="tpu_custom_call" | custom-call | flops 400000000 | bytes 16000000 | tf_op jit(solution)/shard_map/pallas_call | solution.py:346
  26.1 1.2 %shard_map.95 = (f32[256,512]{1,0:T(8,128)}, f32[256,512]{1,0:T(8,128)}, f32[256,512]{1,0:T(8,128)}) custom-call(f32[256,512]{1,0:T(8,128)S(1)} %get-tuple-element.6.h, f32[256,512]{1,0:T(8,128)S(1)} %get-tuple-element.7.m, f32[256,512]{1,0:T(8,128)S(1)} %get-tuple-element.8.n), custom_call_target="tpu_custom_call" | custom-call | bytes 3145728 | tf_op jit(solution)/shard_map/pallas_call | solution.py:376
Async XLA Ops:
  0.6 0.7 %copy-start = (bf16[4,32]{1,0:T(4,128)(2,1)S(1)}, bf16[4,32]{1,0:T(4,128)(2,1)}, u32[]{:S(2)}) copy-start(bf16[4,32]{1,0:T(4,128)(2,1)} %slip_ref.1) | copy-start | bytes 772
  1.3 0.7 %copy-start.1 = (s32[1,9]{1,0:T(1,128)S(1)}, s32[1,9]{1,0:T(1,128)}, u32[]{:S(2)}) copy-start(s32[1,9]{1,0:T(1,128)} %cover_ref.1) | copy-start | bytes 112

commit v3 on v2

--- a/solution.py
+++ b/solution.py
@@ -56,7 +56,7 @@
     n_ox, n_oy,
     slip_ref, green_ref, cover_ref, wet_hbm, h_hbm, m_hbm, n_hbm,
     h_out, m_out, n_out,
-    green, part, h_0, m_0, n_0, h_1, m_1, n_1, wet, fine, spread, edges, terms, terms_t,
+    green, part, h_0, m_0, n_0, h_1, m_1, n_1, wet, fine, spread, terms, terms_t,
     route_x, summed, route_y, row_out, row_in, col_out, col_in,
     green_sem, load_sem, rx_send, rx_recv, ry_send, ry_recv, row_send, row_recv, col_send, col_recv,
 ):
@@ -157,18 +157,25 @@
     lane8 = iota((STRIP, LANES), 1)
     lane = iota((BLOCK, LANES), 1)
 
-    def send_edges(s):
-        for c in range(3):
-            turned = jnp.transpose(edges[c])
-            col_out[s, 0, pl.ds(c, 1)] = turned[:1]
-            col_out[s, 1, pl.ds(c, 1)] = turned[LANES - 1:]
-        when_each(col_copies(s), "start")
-
-    def send_rows(s, state):
+    def send(s, state, packed):
         for c in range(3):
             row_out[s, 0, pl.ds(c, 1)] = state[c][pl.ds(0, 1)]
             row_out[s, 1, pl.ds(c, 1)] = state[c][pl.ds(n_rows - 1, 1)]
+            for t in range(n_rows // LANES):
+                where = pl.ds(t * LANES, LANES)
+                turned = jnp.transpose(packed[c][t])
+                col_out[s, 0, pl.ds(c, 1), where] = turned[:1]
+                col_out[s, 1, pl.ds(c, 1), where] = turned[LANES - 1:]
         when_each(row_copies(s), "start")
+        when_each(col_copies(s), "start")
+        for d in range(2):
+            @pl.when(jnp.logical_not(near[d][0]))
+            def _():
+                row_in[s, d] = row_out[s, d]
+
+            @pl.when(jnp.logical_not(near[2 + d][0]))
+            def _():
+                col_in[s, d] = col_out[s, d]
 
     def matmul(a):
         for q in range(chunks):
@@ -189,7 +196,6 @@
         when_each(route_y_copies(s), "start")
 
     def lift_cells(s):
-        when_each(route_y_copies(s), "wait_recv")
         lift = source * (summed[s, 2] + route_y[s, 0] + route_y[s, 1])
         high = lift.astype(bf16)
         low = (lift - high.astype(f32)).astype(bf16)
@@ -208,7 +214,7 @@
             for b in range(n_blocks)
         ], axis=1)
 
-    def bulk(state, new):
+    def bulk(state, new, wait, beside_last):
         def start(base, down_before):
             quarter, fx, fy = flux_terms(*(field[pl.ds(base, STRIP)] for field in state))
             up = [pltpu.roll(quarter[c] - fx[c], STRIP - 1, 0) for c in range(3)]
@@ -234,22 +240,18 @@
         zero = jnp.zeros((STRIP, n_cols), f32)
         carry = group(0, (None, None, [zero] * 3))
         carry = lax.fori_loop(
-            1, n_strips // GROUP, lambda t, carry: group(pl.multiple_of(t * GROUP * STRIP, GROUP * STRIP), carry), carry
+            1, n_strips // GROUP - 1, lambda t, carry: group(pl.multiple_of(t * GROUP * STRIP, GROUP * STRIP), carry), carry
         )
+        wait()
+        beside_last()
+        carry = group(n_rows - GROUP * STRIP, carry)
         store(n_rows - STRIP, carry[0], carry[1], [zero] * 3)
 
-    def receive(s):
+    def wait_edges(s):
         when_each(row_copies(s), "wait_recv")
         when_each(col_copies(s), "wait_recv")
-        for d in range(2):
-            @pl.when(jnp.logical_not(near[d][0]))
-            def _():
-                row_in[s, d] = row_out[s, d]
-
-            @pl.when(jnp.logical_not(near[2 + d][0]))
-            def _():
-                col_in[s, d] = col_out[s, d]
-
+
+    def receive(s):
         for d in range(2):
             quarter, _, fy = flux_terms(*(col_in[s, d, pl.ds(c, 1)] for c in range(3)))
             for c in range(3):
@@ -266,26 +268,28 @@
                 term = quarter[c] - fx[c] if d else quarter[c] + fx[c]
                 new[c][row] = new[c][row] + (term * dry if c > 0 else term)
 
-        def body(t, carry):
-            where = pl.ds(pl.multiple_of(t * BLOCK, BLOCK), BLOCK)
-            dry_first = wet[where, first_block].astype(f32)
-            dry_last = wet[where, last_block].astype(f32)
-            for b in range(n_cols // LANES):
-                block = pl.ds(b * LANES, LANES)
-                new[0][where, block] = new[0][where, block] + fine[b, where]
+        packed = [[], [], []]
+        for t in range(n_rows // LANES):
+            pieces = [[], [], []]
+            for u in range(LANES // BLOCK):
+                where = pl.ds(t * LANES + u * BLOCK, BLOCK)
+                dry_first = wet[where, first_block].astype(f32)
+                dry_last = wet[where, last_block].astype(f32)
+                for b in range(n_cols // LANES):
+                    block = pl.ds(b * LANES, LANES)
+                    new[0][where, block] = new[0][where, block] + fine[b, where]
+                for c in range(3):
+                    term = terms_t[c, where]
+                    left = jnp.where(lane == 0, term, 0.0)
+                    right = jnp.where(lane == LANES - 1, term, 0.0)
+                    first = new[c][where, first_block] + (left * dry_first if c > 0 else left)
+                    last = new[c][where, last_block] + (right * dry_last if c > 0 else right)
+                    new[c][where, first_block] = first
+                    new[c][where, last_block] = last
+                    pieces[c].append(jnp.where(lane == 0, first, last))
             for c in range(3):
-                term = terms_t[c, where]
-                left = jnp.where(lane == 0, term, 0.0)
-                right = jnp.where(lane == LANES - 1, term, 0.0)
-                first = new[c][where, first_block] + (left * dry_first if c > 0 else left)
-                last = new[c][where, last_block] + (right * dry_last if c > 0 else right)
-                new[c][where, first_block] = first
-                new[c][where, last_block] = last
-                if s < steps - 1:
-                    edges[c, where] = jnp.where(lane == 0, first, last)
-            return carry
-
-        lax.fori_loop(0, n_rows // BLOCK, body, 0)
+                packed[c].append(jnp.concatenate(pieces[c], axis=0))
+        return packed
 
     for a in (2, 0):
         matmul(a)
@@ -294,26 +298,40 @@
 
     for copy in loads:
         copy.wait()
-    for c in range(3):
-        edges[c] = jnp.where(iota((n_rows, LANES), 1) == 0, states[0][c][:, first_block], states[0][c][:, last_block])
-    send_rows(0, states[0])
-    send_edges(0)
+    lane_tile = iota((LANES, LANES), 1)
+    send(0, states[0], [
+        [
+            jnp.where(lane_tile == 0, field[pl.ds(t * LANES, LANES), first_block], field[pl.ds(t * LANES, LANES), last_block])
+            for t in range(n_rows // LANES)
+        ]
+        for field in states[0]
+    ])
 
     matmul(1)
     pass_on(0)
     for s in range(steps):
         state = states[s % 2]
         new = outs if s == steps - 1 else states[1 - s % 2]
-        bulk(state, new)
+
+        def wait():
+            wait_edges(s)
+            if s > 0:
+                when_each(route_y_copies(s), "wait_recv")
+
+        def beside_last():
+            receive(s)
+            if s > 0:
+                lift_cells(s)
+
+        bulk(state, new, wait, beside_last)
         if s == 0:
             for later in range(1, steps):
                 pass_on(later)
-        lift_cells(s)
-        receive(s)
-        finish(s, new)
+            when_each(route_y_copies(0), "wait_recv")
+            lift_cells(0)
+        packed = finish(s, new)
         if s < steps - 1:
-            send_rows(s + 1, new)
-            send_edges(s + 1)
+            send(s + 1, new, packed)
 
     for s in range(steps):
         when_each(route_x_copies(s), "wait_send")
@@ -355,7 +373,6 @@
             pltpu.VMEM((rows, cols), jnp.int32),
             pltpu.VMEM((cols // LANES, rows, LANES), f32),
             pltpu.VMEM((2 * up_cols, cols), bf16),
-            pltpu.VMEM((3, rows, LANES), f32),
             pltpu.VMEM((3, LANES, rows), f32),
             pltpu.VMEM((3, rows, LANES), f32),
             pltpu.VMEM((steps, 2, 3 * up_rows, up_cols), f32),

time: 27.4 us -> 28.1 us (1.026)
  Pallas kernels: 25.3 us -> 25.9 us
    pallas_call x1, Pallas kernels: 24.1 us -> 24.8 us  [shards(): pl.pallas_call(functools.partial(kernel, n_ox, n_oy), out_shape=fields, i...]
where the time goes in v3:
time: 28.1 us; the launch traced here: 27.9 us
  Pallas kernels  25.9 us (92%)
  local copies, waits for them, and re-layouts  1.33 us (5%)
  between operations  0.65 us (2%)
    pallas_call x1, Pallas kernels, shards(): pl.pallas_call(functools.partial(kernel, n_ox, n_oy), out_shape=fields, i...  24.8 us
    unnamed x4, local copies, waits for them, and re-layouts  1.33 us
    pallas_call x1, Pallas kernels, shards(): pl.pallas_call(write_out, out_shape=fields, in_specs=[vmem] * 3, out_spec...  1.17 us

profile of v3, /device:TPU:1, one launch (start us, length us, event | category | flops | bytes accessed | tf_op | source)
XLA Modules:
  0.0 27.9 jit_solution(1981515397429472457)
XLA Ops:
  0.6 0.0 copy-start
  0.6 0.7 %copy-done = bf16[4,32]{1,0:T(4,128)(2,1)S(1)} copy-done((bf16[4,32]{1,0:T(4,128)(2,1)S(1)}, bf16[4,32]{1,0:T(4,128)(2,1)}, u32[]{:S(2)}) %copy-start) | copy-done | bytes 280
  1.3 0.0 copy-start.1
  1.3 0.7 %copy-done.1 = s32[1,9]{1,0:T(1,128)S(1)} copy-done((s32[1,9]{1,0:T(1,128)S(1)}, s32[1,9]{1,0:T(1,128)}, u32[]{:S(2)}) %copy-start.1) | copy-done | bytes 60
  2.0 24.8 %shard_map.94 = (f32[256,512]{1,0:T(8,128)S(1)}, f32[256,512]{1,0:T(8,128)S(1)}, f32[256,512]{1,0:T(8,128)S(1)}) custom-call(bf16[4,32]{1,0:T(4,128)(2,1)S(1)} %copy-done, bf16[9,32,8192]{2,1,0:T(8,128)(2,1)} %bitcast.1, s32[1,9]{1,0:T(1,128)S(1)} %copy-done.1, s32[256,512]{1,0:T(8,128)} %wet_hbm.1, f32[256,512]{1,0:T(8,128)} %h_hbm.1, f32[256,512]{1,0:T(8,128)} %m_hbm.1, ...), custom_call_target="tpu_custom_call" | custom-call | flops 400000000 | bytes 16000000 | tf_op jit(solution)/shard_map/pallas_call | solution.py:364
  26.7 1.2 %shard_map.95 = (f32[256,512]{1,0:T(8,128)}, f32[256,512]{1,0:T(8,128)}, f32[256,512]{1,0:T(8,128)}) custom-call(f32[256,512]{1,0:T(8,128)S(1)} %get-tuple-element.6.h, f32[256,512]{1,0:T(8,128)S(1)} %get-tuple-element.7.m, f32[256,512]{1,0:T(8,128)S(1)} %get-tuple-element.8.n), custom_call_target="tpu_custom_call" | custom-call | bytes 3145728 | tf_op jit(solution)/shard_map/pallas_call | solution.py:393
Async XLA Ops:
  0.6 0.7 %copy-start = (bf16[4,32]{1,0:T(4,128)(2,1)S(1)}, bf16[4,32]{1,0:T(4,128)(2,1)}, u32[]{:S(2)}) copy-start(bf16[4,32]{1,0:T(4,128)(2,1)} %slip_ref.1) | copy-start | bytes 772
  1.3 0.7 %copy-start.1 = (s32[1,9]{1,0:T(1,128)S(1)}, s32[1,9]{1,0:T(1,128)}, u32[]{:S(2)}) copy-start(s32[1,9]{1,0:T(1,128)} %cover_ref.1) | copy-start | bytes 112

commit v4 on v2

--- a/solution.py
+++ b/solution.py
@@ -56,7 +56,7 @@
     n_ox, n_oy,
     slip_ref, green_ref, cover_ref, wet_hbm, h_hbm, m_hbm, n_hbm,
     h_out, m_out, n_out,
-    green, part, h_0, m_0, n_0, h_1, m_1, n_1, wet, fine, spread, edges, terms, terms_t,
+    green, part, h_1, m_1, n_1, wet, fine, spread, edges, terms, terms_t, lhs,
     route_x, summed, route_y, row_out, row_in, col_out, col_in,
     green_sem, load_sem, rx_send, rx_recv, ry_send, ry_recv, row_send, row_recv, col_send, col_recv,
 ):
@@ -64,8 +64,7 @@
     n_rows, n_cols = wet.shape
     up_rows, up_cols = n_rows // COARSE, n_cols // COARSE
     i, j = lax.axis_index("ox"), lax.axis_index("oy")
-    states = ((h_0, m_0, n_0), (h_1, m_1, n_1))
-    outs = (h_out, m_out, n_out)
+    states = ((h_out, m_out, n_out), (h_1, m_1, n_1))
     near = (
         (i > 0, (i - 1, j)),
         (i < n_ox - 1, (i + 1, j)),
@@ -75,19 +74,25 @@
 
     loads = [
         pltpu.make_async_copy(src, dst, load_sem.at[q])
-        for q, (src, dst) in enumerate(((h_hbm, h_0), (m_hbm, m_0), (n_hbm, n_0), (wet_hbm, wet)))
+        for q, (src, dst) in enumerate(((h_hbm, h_out), (m_hbm, m_out), (n_hbm, n_out), (wet_hbm, wet)))
     ]
     chunks = green_sem.shape[1]
     width = green.shape[2] // chunks
-    greens = {}
-    for a in (2, 0, 1):
+
+    def green_copy(a, q):
+        where = (pl.ds(3 * a, 3), slice(None), pl.ds(pl.multiple_of(q * width, width), width))
+        return pltpu.make_async_copy(green_ref.at[where], green.at[where], green_sem.at[a, q])
+
+    def load_slots(o, carry):
+        a = lax.rem(o + 2, 3)
         for q in range(chunks):
-            where = (pl.ds(3 * a, 3), slice(None), pl.ds(q * width, width))
-            greens[a, q] = pltpu.make_async_copy(green_ref.at[where], green.at[where], green_sem.at[a, q])
-            greens[a, q].start()
-        if a == 2:
-            for copy in loads:
-                copy.start()
+            green_copy(a, q).start()
+        return carry
+
+    load_slots(0, 0)
+    for copy in loads:
+        copy.start()
+    lax.fori_loop(1, 3, load_slots, 0)
 
     barrier = pltpu.get_barrier_semaphore()
     for there, device in near:
@@ -113,7 +118,8 @@
     terms[...] = jnp.zeros(terms.shape, f32)
     row_out[...] = jnp.zeros(row_out.shape, f32)
     col_out[...] = jnp.zeros(col_out.shape, f32)
-    lhs = [weights(slip_ref, cover_ref, steps, faults, a) for a in range(3)]
+    for a in range(3):
+        lhs[a] = weights(slip_ref, cover_ref, steps, faults, a)
 
     pl.semaphore_wait(barrier, sum(there.astype(jnp.int32) for there, _ in near))
 
@@ -123,10 +129,14 @@
         )
 
     def when_each(copies, what):
+        sides = {}
         for d, copy in copies:
-            @pl.when(near[d ^ 1 if what == "wait_recv" else d][0])
+            sides.setdefault(d ^ 1 if what == "wait_recv" else d, []).append(copy)
+        for d, some in sides.items():
+            @pl.when(near[d][0])
             def _():
-                getattr(copy, what)()
+                for copy in some:
+                    getattr(copy, what)()
 
     def route_x_copies(s, sides=(0, 1)):
         rows = 3 * up_rows
@@ -157,27 +167,27 @@
     lane8 = iota((STRIP, LANES), 1)
     lane = iota((BLOCK, LANES), 1)
 
-    def send_edges(s):
+    def send(s, state):
         for c in range(3):
+            row_out[s, 0, pl.ds(c, 1)] = state[c][pl.ds(0, 1)]
+            row_out[s, 1, pl.ds(c, 1)] = state[c][pl.ds(n_rows - 1, 1)]
             turned = jnp.transpose(edges[c])
             col_out[s, 0, pl.ds(c, 1)] = turned[:1]
             col_out[s, 1, pl.ds(c, 1)] = turned[LANES - 1:]
-        when_each(col_copies(s), "start")
-
-    def send_rows(s, state):
-        for c in range(3):
-            row_out[s, 0, pl.ds(c, 1)] = state[c][pl.ds(0, 1)]
-            row_out[s, 1, pl.ds(c, 1)] = state[c][pl.ds(n_rows - 1, 1)]
-        when_each(row_copies(s), "start")
+        when_each(row_copies(s) + col_copies(s), "start")
 
     def matmul(a):
-        for q in range(chunks):
-            greens[a, q].wait()
-            block = green[pl.ds(3 * a, 3), :, pl.ds(q * width, width)].reshape(3 * faults, width)
+        def body(q, carry):
+            green_copy(a, q).wait()
+            where = pl.ds(pl.multiple_of(q * width, width), width)
+            block = green[pl.ds(3 * a, 3), :, where].reshape(3 * faults, width)
             out = jnp.dot(lhs[a], block, preferred_element_type=f32)
             for p in range(width // up_cols):
                 row = q * (width // up_cols) + p
                 part[a, pl.ds(row, out.shape[0], stride=up_rows), :] = out[:, p * up_cols:(p + 1) * up_cols]
+            return carry
+
+        lax.fori_loop(0, chunks, body, 0)
 
     def pass_on(s):
         when_each(route_x_copies(s), "wait_recv")
@@ -209,38 +219,37 @@
         ], axis=1)
 
     def bulk(state, new):
-        def start(base, down_before):
+        def rows(base):
             quarter, fx, fy = flux_terms(*(field[pl.ds(base, STRIP)] for field in state))
-            up = [pltpu.roll(quarter[c] - fx[c], STRIP - 1, 0) for c in range(3)]
-            down = [pltpu.roll(quarter[c] + fx[c], 1, 0) for c in range(3)]
-            sides = [beside(quarter[c] - fy[c], quarter[c] + fy[c]) for c in range(3)]
-            acc = [sides[c] + jnp.where(row8 == 0, down_before[c], down[c]) for c in range(3)]
-            return acc, up, down
-
-        def store(base, acc, up, next_up):
-            dry = wet[pl.ds(base, STRIP)].astype(f32)
-            for c in range(3):
-                value = acc[c] + jnp.where(row8 == STRIP - 1, next_up[c], up[c])
-                new[c][pl.ds(base, STRIP)] = value * dry if c > 0 else value
-
-        def group(base, carry):
+            return quarter, fx, fy, [pltpu.roll(quarter[c] - fx[c], STRIP - 1, 0) for c in range(3)]
+
+        def group(t, down_before):
+            first = pl.multiple_of(t * GROUP * STRIP, GROUP * STRIP)
+            now = rows(first)
             for u in range(GROUP):
-                now = start(base + u * STRIP, carry[2])
-                if carry[0] is not None:
-                    store(base + (u - 1) * STRIP, carry[0], carry[1], now[1])
-                carry = now
-            return carry
-
-        zero = jnp.zeros((STRIP, n_cols), f32)
-        carry = group(0, (None, None, [zero] * 3))
-        carry = lax.fori_loop(
-            1, n_strips // GROUP, lambda t, carry: group(pl.multiple_of(t * GROUP * STRIP, GROUP * STRIP), carry), carry
-        )
-        store(n_rows - STRIP, carry[0], carry[1], [zero] * 3)
+                base = first + u * STRIP
+                if u < GROUP - 1:
+                    later = rows(base + STRIP)
+                    next_up = later[3]
+                else:
+                    inside = base + STRIP < n_rows
+                    later = rows(pl.multiple_of(jnp.where(inside, base + STRIP, base), STRIP))
+                    next_up = [jnp.where(inside, value, 0.0) for value in later[3]]
+                quarter, fx, fy, up = now
+                dry = wet[pl.ds(base, STRIP)].astype(f32)
+                down = [pltpu.roll(quarter[c] + fx[c], 1, 0) for c in range(3)]
+                for c in range(3):
+                    value = beside(quarter[c] - fy[c], quarter[c] + fy[c])
+                    value += jnp.where(row8 == 0, down_before[c], down[c])
+                    value += jnp.where(row8 == STRIP - 1, next_up[c], up[c])
+                    new[c][pl.ds(base, STRIP)] = value * dry if c > 0 else value
+                now, down_before = later, down
+            return down_before
+
+        lax.fori_loop(0, n_strips // GROUP, group, [jnp.zeros((STRIP, n_cols), f32)] * 3)
 
     def receive(s):
-        when_each(row_copies(s), "wait_recv")
-        when_each(col_copies(s), "wait_recv")
+        when_each(row_copies(s) + col_copies(s), "wait_recv")
         for d in range(2):
             @pl.when(jnp.logical_not(near[d][0]))
             def _():
@@ -281,45 +290,59 @@
                 last = new[c][where, last_block] + (right * dry_last if c > 0 else right)
                 new[c][where, first_block] = first
                 new[c][where, last_block] = last
-                if s < steps - 1:
-                    edges[c, where] = jnp.where(lane == 0, first, last)
+                edges[c, where] = jnp.where(lane == 0, first, last)
             return carry
 
         lax.fori_loop(0, n_rows // BLOCK, body, 0)
 
-    for a in (2, 0):
+    def slots(o, carry):
+        a = lax.rem(o + 2, 3)
         matmul(a)
-        for s in range(steps):
-            when_each(route_x_copies(s, (a // 2,)), "start")
-
+        for d in range(2):
+            @pl.when(jnp.logical_and(a == 2 * d, near[d][0]))
+            def _():
+                for s in range(steps):
+                    route_x_copies(s, (d,))[0][1].start()
+        return carry
+
+    lax.fori_loop(0, 2, slots, 0)
     for copy in loads:
         copy.wait()
     for c in range(3):
         edges[c] = jnp.where(iota((n_rows, LANES), 1) == 0, states[0][c][:, first_block], states[0][c][:, last_block])
-    send_rows(0, states[0])
-    send_edges(0)
-
-    matmul(1)
+    send(0, states[0])
+    lax.fori_loop(2, 3, slots, 0)
     pass_on(0)
-    for s in range(steps):
-        state = states[s % 2]
-        new = outs if s == steps - 1 else states[1 - s % 2]
-        bulk(state, new)
-        if s == 0:
-            for later in range(1, steps):
-                pass_on(later)
-        lift_cells(s)
-        receive(s)
-        finish(s, new)
-        if s < steps - 1:
-            send_rows(s + 1, new)
-            send_edges(s + 1)
-
-    for s in range(steps):
-        when_each(route_x_copies(s), "wait_send")
-        when_each(route_y_copies(s), "wait_send")
-        when_each(row_copies(s), "wait_send")
-        when_each(col_copies(s), "wait_send")
+
+    def pair(t, carry):
+        for half in range(2):
+            s = 2 * t + half
+            new = states[1 - half]
+            bulk(states[half], new)
+            if half == 0:
+                @pl.when(t == 0)
+                def _():
+                    def later(r, carry):
+                        pass_on(r)
+                        return carry
+
+                    lax.fori_loop(1, steps, later, 0)
+            lift_cells(s)
+            receive(s)
+            finish(s, new)
+            if half == 0:
+                send(s + 1, new)
+            else:
+                @pl.when(t < steps // 2 - 1)
+                def _():
+                    send(s + 1, new)
+        return carry
+
+    lax.fori_loop(0, steps // 2, pair, 0)
+
+    when_each([
+        copy for s in range(steps) for copy in route_x_copies(s) + route_y_copies(s) + row_copies(s) + col_copies(s)
+    ], "wait_send")
 
 
 def write_out(h, m, n, h_hbm, m_hbm, n_hbm, sems):
@@ -351,13 +374,14 @@
         scratch_shapes=[
             pltpu.VMEM((9, faults, green_kernel.shape[2]), bf16),
             pltpu.VMEM((3, part_rows, up_cols), f32),
-        ] + [pltpu.VMEM((rows, cols), f32)] * 6 + [
+        ] + [pltpu.VMEM((rows, cols), f32)] * 3 + [
             pltpu.VMEM((rows, cols), jnp.int32),
             pltpu.VMEM((cols // LANES, rows, LANES), f32),
             pltpu.VMEM((2 * up_cols, cols), bf16),
             pltpu.VMEM((3, rows, LANES), f32),
             pltpu.VMEM((3, LANES, rows), f32),
             pltpu.VMEM((3, rows, LANES), f32),
+            pltpu.VMEM((3, part_rows // up_rows, 3 * faults), bf16),
             pltpu.VMEM((steps, 2, 3 * up_rows, up_cols), f32),
             pltpu.VMEM((steps, 3, up_rows, up_cols), f32),
             pltpu.VMEM((steps, 2, up_rows, up_cols), f32),

time: 27.4 us -> 27.8 us (1.015)
  Pallas kernels: 25.3 us -> 25.7 us
    pallas_call x1, Pallas kernels: 24.1 us -> 24.5 us  [shards(): pl.pallas_call(functools.partial(kernel, n_ox, n_oy), out_shape=fields, i...]
where the time goes in v4:
time: 27.8 us; the launch traced here: 27.6 us
  Pallas kernels  25.7 us (92%)
  local copies, waits for them, and re-layouts  1.33 us (5%)
  between operations  0.65 us (2%)
    pallas_call x1, Pallas kernels, shards(): pl.pallas_call(functools.partial(kernel, n_ox, n_oy), out_shape=fields, i...  24.5 us
    unnamed x4, local copies, waits for them, and re-layouts  1.33 us
    pallas_call x1, Pallas kernels, shards(): pl.pallas_call(write_out, out_shape=fields, in_specs=[vmem] * 3, out_spec...  1.17 us

profile of v4, /device:TPU:1, one launch (start us, length us, event | category | flops | bytes accessed | tf_op | source)
XLA Modules:
  0.0 27.6 jit_solution(9840514123053541383)
XLA Ops:
  0.6 0.0 copy-start
  0.6 0.7 %copy-done = bf16[4,32]{1,0:T(4,128)(2,1)S(1)} copy-done((bf16[4,32]{1,0:T(4,128)(2,1)S(1)}, bf16[4,32]{1,0:T(4,128)(2,1)}, u32[]{:S(2)}) %copy-start) | copy-done | bytes 280
  1.3 0.0 copy-start.1
  1.3 0.7 %copy-done.1 = s32[1,9]{1,0:T(1,128)S(1)} copy-done((s32[1,9]{1,0:T(1,128)S(1)}, s32[1,9]{1,0:T(1,128)}, u32[]{:S(2)}) %copy-start.1) | copy-done | bytes 60
  2.0 24.5 %shard_map.94 = (f32[256,512]{1,0:T(8,128)S(1)}, f32[256,512]{1,0:T(8,128)S(1)}, f32[256,512]{1,0:T(8,128)S(1)}) custom-call(bf16[4,32]{1,0:T(4,128)(2,1)S(1)} %copy-done, bf16[9,32,8192]{2,1,0:T(8,128)(2,1)} %bitcast.1, s32[1,9]{1,0:T(1,128)S(1)} %copy-done.1, s32[256,512]{1,0:T(8,128)} %wet_hbm.1, f32[256,512]{1,0:T(8,128)} %h_hbm.1, f32[256,512]{1,0:T(8,128)} %m_hbm.1, ...), custom_call_target="tpu_custom_call" | custom-call | flops 400000000 | bytes 16000000 | tf_op jit(solution)/shard_map/pallas_call | solution.py:369
  26.5 1.2 %shard_map.95 = (f32[256,512]{1,0:T(8,128)}, f32[256,512]{1,0:T(8,128)}, f32[256,512]{1,0:T(8,128)}) custom-call(f32[256,512]{1,0:T(8,128)S(1)} %get-tuple-element.6.h, f32[256,512]{1,0:T(8,128)S(1)} %get-tuple-element.7.m, f32[256,512]{1,0:T(8,128)S(1)} %get-tuple-element.8.n), custom_call_target="tpu_custom_call" | custom-call | bytes 3145728 | tf_op jit(solution)/shard_map/pallas_call | solution.py:400
Async XLA Ops:
  0.6 0.7 %copy-start = (bf16[4,32]{1,0:T(4,128)(2,1)S(1)}, bf16[4,32]{1,0:T(4,128)(2,1)}, u32[]{:S(2)}) copy-start(bf16[4,32]{1,0:T(4,128)(2,1)} %slip_ref.1) | copy-start | bytes 772
  1.3 0.7 %copy-start.1 = (s32[1,9]{1,0:T(1,128)S(1)}, s32[1,9]{1,0:T(1,128)}, u32[]{:S(2)}) copy-start(s32[1,9]{1,0:T(1,128)} %cover_ref.1) | copy-start | bytes 112

commit v5 on v2

--- a/solution.py
+++ b/solution.py
@@ -287,27 +287,27 @@
 
         lax.fori_loop(0, n_rows // BLOCK, body, 0)
 
-    for a in (2, 0):
-        matmul(a)
-        for s in range(steps):
-            when_each(route_x_copies(s, (a // 2,)), "start")
-
+    matmul(2)
     for copy in loads:
         copy.wait()
     for c in range(3):
         edges[c] = jnp.where(iota((n_rows, LANES), 1) == 0, states[0][c][:, first_block], states[0][c][:, last_block])
     send_rows(0, states[0])
     send_edges(0)
-
+    when_each(route_x_copies(0, (1,)), "start")
+    matmul(0)
+    when_each(route_x_copies(0, (0,)), "start")
+    when_each(route_x_copies(1), "start")
     matmul(1)
     pass_on(0)
     for s in range(steps):
         state = states[s % 2]
         new = outs if s == steps - 1 else states[1 - s % 2]
         bulk(state, new)
-        if s == 0:
-            for later in range(1, steps):
-                pass_on(later)
+        if s + 1 < steps:
+            pass_on(s + 1)
+        if s + 2 < steps:
+            when_each(route_x_copies(s + 2), "start")
         lift_cells(s)
         receive(s)
         finish(s, new)

time: 27.4 us -> 26.5 us (0.967)
  Pallas kernels: 25.3 us -> 24.4 us
    pallas_call x1, Pallas kernels: 24.1 us -> 23.2 us  [shards(): pl.pallas_call(functools.partial(kernel, n_ox, n_oy), out_shape=fields, i...]
where the time goes in v5:
time: 26.5 us; the launch traced here: 26.4 us
  Pallas kernels  24.4 us (92%)
  local copies, waits for them, and re-layouts  1.33 us (5%)
  between operations  0.65 us (2%)
    pallas_call x1, Pallas kernels, shards(): pl.pallas_call(functools.partial(kernel, n_ox, n_oy), out_shape=fields, i...  23.2 us
    unnamed x4, local copies, waits for them, and re-layouts  1.33 us
    pallas_call x1, Pallas kernels, shards(): pl.pallas_call(write_out, out_shape=fields, in_specs=[vmem] * 3, out_spec...  1.17 us

profile of v5, /device:TPU:1, one launch (start us, length us, event | category | flops | bytes accessed | tf_op | source)
XLA Modules:
  0.0 26.4 jit_solution(15597985717101629259)
XLA Ops:
  0.6 0.0 copy-start
  0.6 0.7 %copy-done = bf16[4,32]{1,0:T(4,128)(2,1)S(1)} copy-done((bf16[4,32]{1,0:T(4,128)(2,1)S(1)}, bf16[4,32]{1,0:T(4,128)(2,1)}, u32[]{:S(2)}) %copy-start) | copy-done | bytes 280
  1.3 0.0 copy-start.1
  1.3 0.7 %copy-done.1 = s32[1,9]{1,0:T(1,128)S(1)} copy-done((s32[1,9]{1,0:T(1,128)S(1)}, s32[1,9]{1,0:T(1,128)}, u32[]{:S(2)}) %copy-start.1) | copy-done | bytes 60
  2.0 23.2 %shard_map.94 = (f32[256,512]{1,0:T(8,128)S(1)}, f32[256,512]{1,0:T(8,128)S(1)}, f32[256,512]{1,0:T(8,128)S(1)}) custom-call(bf16[4,32]{1,0:T(4,128)(2,1)S(1)} %copy-done, bf16[9,32,8192]{2,1,0:T(8,128)(2,1)} %bitcast.1, s32[1,9]{1,0:T(1,128)S(1)} %copy-done.1, s32[256,512]{1,0:T(8,128)} %wet_hbm.1, f32[256,512]{1,0:T(8,128)} %h_hbm.1, f32[256,512]{1,0:T(8,128)} %m_hbm.1, ...), custom_call_target="tpu_custom_call" | custom-call | flops 400000000 | bytes 16000000 | tf_op jit(solution)/shard_map/pallas_call | solution.py:346
  25.2 1.2 %shard_map.95 = (f32[256,512]{1,0:T(8,128)}, f32[256,512]{1,0:T(8,128)}, f32[256,512]{1,0:T(8,128)}) custom-call(f32[256,512]{1,0:T(8,128)S(1)} %get-tuple-element.6.h, f32[256,512]{1,0:T(8,128)S(1)} %get-tuple-element.7.m, f32[256,512]{1,0:T(8,128)S(1)} %get-tuple-element.8.n), custom_call_target="tpu_custom_call" | custom-call | bytes 3145728 | tf_op jit(solution)/shard_map/pallas_call | solution.py:376
Async XLA Ops:
  0.6 0.7 %copy-start = (bf16[4,32]{1,0:T(4,128)(2,1)S(1)}, bf16[4,32]{1,0:T(4,128)(2,1)}, u32[]{:S(2)}) copy-start(bf16[4,32]{1,0:T(4,128)(2,1)} %slip_ref.1) | copy-start | bytes 772
  1.3 0.7 %copy-start.1 = (s32[1,9]{1,0:T(1,128)S(1)}, s32[1,9]{1,0:T(1,128)}, u32[]{:S(2)}) copy-start(s32[1,9]{1,0:T(1,128)} %cover_ref.1) | copy-start | bytes 112
